TPU v7x, 32 devices: a whole 2x2x4 slice. The times are simulated.
32 devices in a mesh: ctx: 4 (over x, core), wide: 8 (over z, y).
Axes of the slice: x: 2, y: 2, z: 4, core: 2. Of those that a mesh axis runs over, the one named last changes fastest.
Arguments:
- tokens: bfloat16 [4096, 2688], P(('ctx', 'wide')), may hold values from -10 to 10
- mamba_gain: float32 [2688], replicated, may hold values from 0.25 to 1.75
- w_z: bfloat16 [2688, 4096], P(None, 'wide'), may hold values from -0.125 to 0.125
- w_x: bfloat16 [2688, 4096], P(None, 'wide'), may hold values from -0.125 to 0.125
- w_bc: bfloat16 [2688, 2048], P(None, 'wide'), may hold values from -0.125 to 0.125
- w_dt: bfloat16 [2688, 64], replicated, may hold values from -1 to 1
- dt_bias: float32 [64], P('wide'), may hold values from -2 to 0
- a_log: float32 [64], P('wide')
- conv_x: float32 [4, 4096], P(None, 'wide'), may hold values from -3 to 3
- conv_bc: float32 [4, 2048], replicated, may hold values from -3 to 3
- skip: float32 [64], P('wide'), may hold values from 0.5 to 1.5
- norm_gain: float32 [4096], P('wide'), may hold values from 0.25 to 1.75
- w_out: bfloat16 [4096, 2688], P('wide'), may hold values from -0.09375 to 0.09375
- moe_gain: float32 [2688], replicated, may hold values from 0.25 to 1.75
- expert_ids: int32 [4096, 6], P(('ctx', 'wide')), may hold values from 0 to 31, all different within a row; in each aligned block of 128 rows (0 to 127, 128 to 255, ...) at most 28 rows name the same one
- router_weights: float32 [4096, 6], P(('ctx', 'wide')), may hold values from 0.05 to 0.5
- w_up: bfloat16 [32, 2688, 1856], P(('ctx', 'wide')), may hold values from -0.125 to 0.125
- w_down: bfloat16 [32, 1856, 2688], P(('ctx', 'wide')), may hold values from -0.125 to 0.125
Outputs:
- mixed: bfloat16 [4096, 2688], P(('ctx', 'wide'))
Inputs may be any that keep to these rules, and one draw needn't show every extreme that they name: `expert_ids`: within the rows of one device (128 tokens), no expert is named more than 28 times, and a row names 6 different experts.
All inputs are finite; a program needn't handle non-finite values.
Results may differ from a plain program's by a relative error of at most 0.015.
Values may be sent and summed in bfloat16 or wider, within the bound.
No kernel may reach another device: no remote copies, remote signals or barrier semaphores. Data moves between devices by JAX's collectives and lax.ppermute only.
A program may use at most 128 MiB of HBM per device.

v0:
```python
import jax
import jax.numpy as jnp
from jax import lax
from jax.sharding import PartitionSpec as P

STATE = 128
GROUPS = 8
KERNEL = 4
TOP = 6
EXP_DEV = 1
BLOCK = 128


EPSILON = 1e-05
PRECISE = lax.Precision.HIGHEST


def partner_2(block, axis, bit):
    count = lax.axis_size(axis)
    route = []
    for low in range(count):
        high = low | 1 << bit
        if high != low and high < count:
            route += [(low, high), (high, low)]
    return lax.ppermute(block, axis, route)


def shifted(block, axis, distance):
    devices = range(lax.axis_size(axis))
    route = [(i - distance, i) for i in devices if i - distance in devices]
    return lax.ppermute(block, axis, route)


def prefix(part, axis, combine, identity):
    place = lax.axis_index(axis)
    gathered = jax.tree.map(lambda a: lax.all_gather(a, axis), part)
    state = jax.tree.map(lambda a, e: jnp.zeros_like(a) + jnp.asarray(e, a.dtype), part, identity)

    def one(lap, state):
        return combine(
            state, jax.tree.map(lambda a: lax.dynamic_index_in_dim(a, lap, 0, False), gathered)
        )

    return lax.fori_loop(0, place, one, state)


def rms_scale(values, gain_vec):
    mean_sq = jnp.mean(values * values, axis=-1, keepdims=True)
    return values * lax.rsqrt(mean_sq + EPSILON) * gain_vec


def slot_numbers(flat_ids, experts):
    onehot = (flat_ids[:, None] == jnp.arange(experts, dtype=jnp.int32)[None, :]).astype(jnp.int32)
    before = jnp.cumsum(onehot, axis=0) - onehot
    return jnp.sum(before * onehot, axis=1)


def expert_apply(arrived, w_up, w_down):
    model_width = arrived.shape[2]
    slot_count = arrived.shape[1]
    grouped = arrived.reshape(-1, EXP_DEV, slot_count, model_width)
    up_proj = jnp.einsum("secd,edf->secf", grouped, w_up, preferred_element_type=jnp.float32)
    activated = jax.nn.relu(up_proj)
    activated = (activated * activated).astype(jnp.bfloat16)
    expert_out = jnp.einsum(
        "secf,efd->secd", activated, w_down, preferred_element_type=jnp.float32
    ).astype(jnp.bfloat16)
    return expert_out.reshape(arrived.shape)


def shards(
    tokens,
    mamba_gain,
    w_z,
    w_x,
    w_bc,
    w_dt,
    dt_bias,
    a_log,
    conv_x,
    conv_bc,
    skip,
    norm_gain,
    w_out,
    moe_gain,
    expert_ids,
    router_weights,
    w_up,
    w_down,
):
    wide_count = lax.axis_size("wide")
    ctx_count = lax.axis_size("ctx")
    tok_rows, model_width = tokens.shape
    heads_here = dt_bias.shape[0]
    inner_here = w_z.shape[1]
    head_dim = inner_here // heads_here
    stream = tokens.astype(jnp.float32)
    normed = rms_scale(stream, mamba_gain).astype(jnp.bfloat16)
    merged_weight = jnp.concatenate([w_z, w_x, w_bc], 1)
    projected = jnp.dot(
        lax.all_gather(normed, "wide", axis=0, tiled=True),
        merged_weight,
        preferred_element_type=jnp.float32,
    ).astype(jnp.bfloat16)
    gate_in = projected[:, :inner_here]
    x_in = projected[:, inner_here : 2 * inner_here]
    bc_share = projected[:, 2 * inner_here :]
    raw_steps = jnp.dot(normed, w_dt, preferred_element_type=jnp.float32)
    steps_here = lax.all_to_all(raw_steps, "wide", split_axis=1, concat_axis=0, tiled=True)
    position = lax.axis_index("wide")
    members = wide_count // GROUPS
    for bit_number in range(members.bit_length() - 1):
        partner = partner_2(bc_share, "wide", bit_number)
        upper_half = position // 2**bit_number % 2
        bc_share = jnp.where(
            upper_half == 1,
            jnp.concatenate([partner, bc_share], 1),
            jnp.concatenate([bc_share, partner], 1),
        )
    group_index = position // members
    taps_group = lax.dynamic_slice_in_dim(conv_bc, group_index * 2 * STATE, 2 * STATE, 1)
    pre_conv = jnp.concatenate([x_in, bc_share], 1)
    rim_rows = shifted(pre_conv[-(KERNEL - 1) :], "ctx", 1)
    extended = jnp.concatenate([rim_rows, pre_conv], 0).astype(jnp.float32)
    conv_taps = jnp.concatenate([conv_x, taps_group], 1)
    span_rows = pre_conv.shape[0]
    total = jnp.zeros(pre_conv.shape, jnp.float32)
    for offset in range(KERNEL):
        total = total + conv_taps[offset] * extended[offset : offset + span_rows]
    conved = jax.nn.silu(total)
    x_conv = conved[:, :inner_here]
    b_conv = conved[:, inner_here : inner_here + STATE]
    c_conv = conved[:, inner_here + STATE :]
    step_size = jax.nn.softplus(steps_here + dt_bias)
    log_decay = -jnp.exp(a_log) * step_size
    blocks = span_rows // BLOCK
    x_blocks = x_conv.reshape(blocks, BLOCK, heads_here, head_dim)
    b_blocks = b_conv.reshape(blocks, BLOCK, STATE)
    c_blocks = c_conv.reshape(blocks, BLOCK, STATE)
    step_blocks = step_size.reshape(blocks, BLOCK, heads_here)
    cum_decay = jnp.cumsum(log_decay.reshape(blocks, BLOCK, heads_here), axis=1)
    scores = jnp.einsum("nis,njs->nij", c_blocks, b_blocks, precision=PRECISE)
    cum_heads = jnp.transpose(cum_decay, (0, 2, 1))
    gap_decay = cum_heads[:, :, :, None] - cum_heads[:, :, None, :]
    causal = jnp.arange(BLOCK)[:, None] >= jnp.arange(BLOCK)[None, :]
    decay_mask = jnp.exp(jnp.where(causal[None, None], gap_decay, -jnp.inf))
    weights = scores[:, None] * decay_mask * jnp.transpose(step_blocks, (0, 2, 1))[:, :, None, :]
    y_intra = jnp.einsum("nhij,njhp->nihp", weights, x_blocks, precision=PRECISE)
    tail_factor = jnp.exp(cum_decay[:, -1:, :] - cum_decay) * step_blocks
    block_states = jnp.einsum(
        "njh,njhp,njs->nhps", tail_factor, x_blocks, b_blocks, precision=PRECISE
    )
    block_decay = jnp.exp(cum_decay[:, -1, :])

    def advance(carry, item):
        carried, decay_before = carry
        state_block, decay_block = item
        return (
            (decay_block[:, None, None] * carried + state_block, decay_before * decay_block),
            (carried, decay_before),
        )

    zero_state = jnp.zeros((heads_here, head_dim, STATE), jnp.float32)
    (span_state, span_decay), (starts, decays_before) = lax.scan(
        advance, (zero_state, jnp.ones((heads_here,), jnp.float32)), (block_states, block_decay)
    )

    def join_states(earlier, later):
        return (earlier[0] * later[0], later[0][:, None, None] * earlier[1] + later[1])

    prior_state = prefix(
        (span_decay, span_state),
        "ctx",
        join_states,
        (jnp.ones_like(span_decay), jnp.zeros_like(span_state)),
    )
    incoming = prior_state[1]
    starts = starts + decays_before[:, :, None, None] * incoming[None]
    y_inter = jnp.exp(cum_decay)[..., None] * jnp.einsum(
        "nis,nhps->nihp", c_blocks, starts, precision=PRECISE
    )
    y_total = (y_intra + y_inter).reshape(span_rows, heads_here, head_dim)
    y_total = y_total + skip[:, None] * x_conv.reshape(span_rows, heads_here, head_dim)
    gated = y_total * jax.nn.silu(gate_in.astype(jnp.float32)).reshape(
        span_rows, heads_here, head_dim
    )
    gated = gated * lax.rsqrt(jnp.mean(gated * gated, axis=-1, keepdims=True) + EPSILON)
    gated = (gated.reshape(span_rows, inner_here) * norm_gain).astype(jnp.bfloat16)
    mamba_out = lax.psum_scatter(
        jnp.dot(gated, w_out, preferred_element_type=jnp.float32).astype(jnp.bfloat16),
        "wide",
        scatter_dimension=0,
        tiled=True,
    ).astype(jnp.float32)
    hidden_stream = (stream + mamba_out).astype(jnp.bfloat16)
    hidden_f32 = hidden_stream.astype(jnp.float32)
    moe_in = rms_scale(hidden_f32, moe_gain).astype(jnp.bfloat16)
    experts = EXP_DEV * ctx_count * wide_count
    capacity = max(2, (7 * tok_rows * TOP + 6 * experts - 1) // (6 * experts))
    flat_ids = expert_ids.reshape(-1)
    slots = slot_numbers(flat_ids, experts)
    slot_index = flat_ids * capacity + slots
    repeated = jnp.repeat(moe_in, TOP, axis=0)
    outgoing = (
        jnp.zeros((experts * capacity, model_width), jnp.bfloat16).at[slot_index].set(repeated)
    )
    outgoing = outgoing.reshape(experts, capacity, model_width)
    returned = lax.all_to_all(
        expert_apply(
            lax.all_to_all(outgoing, ("ctx", "wide"), split_axis=0, concat_axis=0, tiled=True),
            w_up,
            w_down,
        ),
        ("ctx", "wide"),
        split_axis=0,
        concat_axis=0,
        tiled=True,
    )
    picked = returned.reshape(experts * capacity, model_width)[slot_index].reshape(
        tok_rows, TOP, model_width
    )
    combined = jnp.einsum("tk,tkd->td", router_weights, picked.astype(jnp.float32))
    return (hidden_f32 + combined).astype(jnp.bfloat16)


def solution(mesh):
    placed = (
        P(("ctx", "wide"), None),
        P(),
        P(None, "wide"),
        P(None, "wide"),
        P(None, "wide"),
        P(),
        P("wide"),
        P("wide"),
        P(None, "wide"),
        P(),
        P("wide"),
        P("wide"),
        P("wide", None),
        P(),
        P(("ctx", "wide"), None),
        P(("ctx", "wide"), None),
        P(("ctx", "wide"), None, None),
        P(("ctx", "wide"), None, None),
    )
    return jax.shard_map(
        shards, mesh=mesh, in_specs=placed, out_specs=P(("ctx", "wide"), None), check_vma=False
    )
```

profile of v0, /device:TPU:0, one launch (start us, length us, event | category | flops | bytes accessed | tf_op | source)
XLA Modules:
  0.0 702.2 jit_solution(12375089743203692186)
XLA Ops:
  12.4 7.3 %all-to-all-start = ((f32[128,8,8]{0,2,1:T(8,128)}), f32[128,8,8]{0,2,1:T(8,128)}, u32[]{:S(2)}, u32[]{:S(2)}) async-start(f32[128,8,8]{0,2,1:T(8,128)} %convolution_bitcast_fusion), calls=%async_computation | async-start | bytes 65536 | tf_op jit(solution)/shard_map/all_to_all | solution.py:109
  21.0 5.6 all-to-all-done
  31.4 71.1 %all-gather.5.cloned.1.call-done = bf16[1024,2688]{1,0:T(8,128)(2,1)} async-done(((bf16[128,2688]{1,0:T(8,128)(2,1)}), bf16[1024,2688]{1,0:T(8,128)(2,1)}) %all-gather.5.cloned.1.call-update) | async-done | bytes 5505040 | tf_op jit(solution)/shard_map/all_gather | solution.py:101
  102.6 12.2 %fusion.31 = bf16[1024,1280]{1,0:T(8,128)(2,1)S(1)} fusion(bf16[1024,2688]{1,0:T(8,128)(2,1)} %all-gather.5.cloned.1.call-done, bf16[2688,256]{1,0:T(8,128)(2,1)} %param.26, bf16[2688,512]{1,0:T(8,128)(2,1)} %param.25, bf16[2688,512]{1,0:T(8,128)(2,1)} %param.24), kind=kOutput, calls=%fused_computation.31 | convolution fusion | flops 7068385280 | bytes 15007744 | tf_op jit(solution)/shard_map/dot_general | solution.py:100
  139.7 20.1 %while.30 = (s32[]{:T(128)}, f32[8,64,128]{2,1,0:T(8,128)S(1)}, f32[8]{0:T(128)S(1)}, f32[8,8,64,128]{3,2,1,0:T(8,128)}, f32[8,8]{1,0:T(8,128)S(1)}, /*index=5*/...) while((s32[]{:T(128)}, f32[8,64,128]{2,1,0:T(8,128)S(1)}, f32[8]{0:T(128)S(1)}, ...), condition=%wide.region_3.4_spmd.clone, body=%wide.region_2.3_spmd.clone.sunk | while | flops 262163 | bytes 1311605 | solution.py:164
  174.9 7.3 %all-reduce = f32[32]{0:T(128)S(1)} all-reduce(f32[32]{0:T(128)S(1)} %dynamic-update-slice), channel_id=2, replica_groups=mesh['ctx'=4,'wide'=8] {'ctx'}, use_global_device_ids=true, to_apply=%add | all-reduce | flops 32 | bytes 256
  184.5 10.8 %fusion.17 = f32[8,8,64,128]{3,2,1,0:T(8,128)} fusion(f32[8,128,8,64]{1,0,3,2:T(8,128)} %bitcast.151, f32[8,8,128]{2,1,0:T(8,128)S(1)} %copy.73, f32[8,8,128]{2,1,0:T(8,128)S(1)} %copy.71, f32[8,128,128]{2,1,0:T(8,128)S(1)} %fusion.104, pred[128,128]{1,0:T(8,128)(4,1)S(1)} %iota_compare_fusion.2), kind=kOutput, calls=%fused_computation.25 | convolution fusion | flops 809500672 | bytes 4800512 | tf_op jit(solution)/shard_map/nhij,njhp->nihp/dot_general | solution.py:148
  195.7 5.5 bitcast_add_fusion.3
  201.2 3.8 copy.94
  205.0 4.8 reshape.217
  218.0 9.2 %convolution_convert_fusion = bf16[1024,2688]{1,0:T(8,128)(2,1)} fusion(bf16[512,2688]{1,0:T(8,128)(2,1)S(1)} %copy-done, f32[1024,512]{1,0:T(8,128)} %copy.83, f32[1024,512]{1,0:T(8,128)} %reshape.217, f32[512]{0:T(512)S(1)} %copy-done.21, f32[512]{0:T(512)S(1)} %mul.269, f32[1024,768]{1,0:T(8,128)} %copy-done.4, bf16[1024,1280]{1,0:T(8,128)(2,1)} %copy-done.6), kind=kOutput, calls=%fused_computation.22 | convolution fusion | flops 2827091968 | bytes 15601664 | tf_op jit(solution)/shard_map/dot_general | solution.py:190
  230.7 103.9 %reduce-scatter.2.cloned.1.call-done = bf16[128,2688]{1,0:T(8,128)(2,1)} async-done(((bf16[1024,2688]{1,0:T(8,128)(2,1)}), bf16[128,2688]{1,0:T(8,128)(2,1)}) %reduce-scatter.2.cloned.1.call-update) | async-done | bytes 688144 | tf_op jit(solution)/shard_map/reduce_scatter | solution.py:189
  340.5 7.4 %reshape.200 = bf16[768,2688]{1,0:T(8,128)(2,1)} reshape(bf16[128,6,2688]{2,1,0:T(8,128)(2,1)} %broadcast_in_dim.36) | data formatting | bytes 8257536 | tf_op jit(solution)/shard_map/reshape | solution.py:203
  347.8 12.5 %scatter_custom_fusion = bf16[896,2688]{1,0:T(8,128)(2,1)} fusion(s32[768]{0:T(1024)S(1)} %fusion.87, bf16[768,2688]{1,0:T(8,128)(2,1)} %reshape.200, bf16[]{:T(256)} %constant.93.clone.1), kind=kCustom, calls=%fused_computation.43 | custom fusion | bytes 4817408 | tf_op jit(solution)/shard_map/scatter | solution.py:205
  360.3 7.3 %reshape.183 = bf16[32,28,2688]{2,1,0:T(8,128)(2,1)} reshape(bf16[896,2688]{1,0:T(8,128)(2,1)} %scatter_custom_fusion) | data formatting | bytes 9633792 | tf_op jit(solution)/shard_map/reshape | solution.py:207
  367.6 127.7 %all_to_all.23 = bf16[32,28,2688]{2,1,0:T(8,128)(2,1)} all-to-all(bf16[32,28,2688]{2,1,0:T(8,128)(2,1)} %reshape.183), channel_id=1, replica_groups=mesh['ctx'=4,'wide'=8] {'ctx','wide'}, dimensions={0} | all-to-all | bytes 9633792 | tf_op jit(solution)/shard_map/all_to_all | solution.py:210
  495.3 33.2 %fusion.13 = bf16[32,28,2688]{2,0,1:T(8,128)(2,1)} fusion(bf16[1,1856,2688]{2,1,0:T(8,128)(2,1)} %param.39, bf16[1,2688,1856]{1,2,0:T(8,128)(2,1)} %param.38, bf16[32,28,2688]{2,1,0:T(8,128)(2,1)} %all_to_all.23), kind=kOutput, calls=%fused_computation.23 | convolution fusion | flops 17887715328 | bytes 29589504 | tf_op jit(solution)/shard_map/secf,efd->secd/dot_general | solution.py:65
  528.5 6.3 copy.89
  534.8 3.7 all-to-all-start.2
  538.7 124.9 %all-to-all-done.2 = bf16[32,28,2688]{2,1,0:T(8,128)(2,1)} async-done(((bf16[32,28,2688]{2,1,0:T(8,128)(2,1)}), bf16[32,28,2688]{2,1,0:T(8,128)(2,1)}, u32[]{:S(2)}, u32[]{:S(2)}) %all-to-all-start.2) | async-done | bytes 4816928 | tf_op jit(solution)/shard_map/all_to_all | solution.py:208
  663.6 7.4 %reshape.186 = bf16[896,2688]{1,0:T(8,128)(2,1)} reshape(bf16[32,28,2688]{2,1,0:T(8,128)(2,1)} %all-to-all-done.2) | data formatting | bytes 9633792 | tf_op jit(solution)/shard_map/reshape | solution.py:219
  670.9 11.8 %gather_fusion = bf16[768,2688]{1,0:T(8,128)(2,1)} fusion(bf16[896,2688]{1,0:T(8,128)(2,1)} %reshape.186, s32[1024]{0:T(1024)S(1)} %pad_clamp_fusion), kind=kCustom, calls=%fused_computation | custom fusion | bytes 8260608 | tf_op jit(solution)/shard_map/gather | solution.py:219
  682.7 7.3 %reshape.187 = bf16[128,6,2688]{2,1,0:T(8,128)(2,1)} reshape(bf16[768,2688]{1,0:T(8,128)(2,1)} %gather_fusion) | data formatting | bytes 8257536 | tf_op jit(solution)/shard_map/reshape | solution.py:219
  690.0 4.3 fusion.105
  (154 shorter events, 92.5 us)
Async XLA Ops:
  6.5 211.4 %copy-start = (bf16[512,2688]{1,0:T(8,128)(2,1)S(1)}, bf16[512,2688]{1,0:T(8,128)(2,1)}, u32[]{:S(2)}) copy-start(bf16[512,2688]{1,0:T(8,128)(2,1)} %param.34) | copy-start | bytes 8257540
  6.5 3.7 copy-start.11
  6.5 13.2 %copy-start.22 = (f32[8]{0:T(128)S(1)}, f32[8]{0:T(128)}, u32[]{:S(2)}) copy-start(f32[8]{0:T(128)} %param.29) | copy-start | bytes 100
  6.5 14.4 %copy-start.16 = (f32[4,512]{1,0:T(4,128)S(1)}, f32[4,512]{1,0:T(4,128)}, u32[]{:S(2)}) copy-start(f32[4,512]{1,0:T(4,128)} %param.30) | copy-start | bytes 24580
  6.5 96.0 %all-gather.5.cloned.1.call-start = ((), (), s32[]{:S(2)}) async-start(), calls=%async_computation.4 | async-start | bytes 6193152 | tf_op jit(solution)/shard_map/all_gather | solution.py:101
  12.4 14.2 %all-to-all-start = ((f32[128,8,8]{0,2,1:T(8,128)}), f32[128,8,8]{0,2,1:T(8,128)}, u32[]{:S(2)}, u32[]{:S(2)}) async-start(f32[128,8,8]{0,2,1:T(8,128)} %convolution_bitcast_fusion), calls=%async_computation | async-start | bytes 65536 | tf_op jit(solution)/shard_map/all_to_all | solution.py:109
  19.7 175.6 %all-gather.7.cloned.1.call-start = ((), (), s32[]{:S(2)}) async-start(), calls=%async_computation.6 | async-start | bytes 1310720 | tf_op jit(solution)/shard_map/all_gather | solution.py:36
  116.9 5.1 collective-permute-start
  126.4 2.3 copy-start.4
  132.8 2.1 copy-start.12
  134.8 4.9 copy-start.5
  135.0 4.7 copy-start.14
  135.0 4.7 copy-start.18
  139.7 24.8 %copy-start.17 = (f32[8]{0:T(128)S(1)}, f32[8]{0:T(128)}, u32[]{:S(2)}) copy-start(f32[8]{0:T(128)} %param.28) | copy-start | bytes 100
  160.5 174.1 %reduce-scatter.2.cloned.1.call-start = ((), (), s32[]{:S(2)}) async-start(), calls=%async_computation.5 | async-start | bytes 6193152 | tf_op jit(solution)/shard_map/reduce_scatter | solution.py:189
  171.7 10.5 %copy-start.9 = (f32[1024,128]{1,0:T(8,128)S(1)}, f32[1024,128]{1,0:T(8,128)}, u32[]{:S(2)}) copy-start(f32[1024,128]{1,0:T(8,128)} %get-tuple-element.150) | copy-start | bytes 1572868
  205.0 4.8 copy-start.20
  215.0 3.0 copy-start.21
  227.2 107.5 %copy-start.3 = (bf16[128,2688]{1,0:T(8,128)(2,1)S(1)}, bf16[128,2688]{1,0:T(8,128)(2,1)}, u32[]{:S(2)}) copy-start(bf16[128,2688]{1,0:T(8,128)(2,1)} %param.22) | copy-start | bytes 2064388
  227.2 108.9 %copy-start.15 = (f32[2688]{0:T(1024)S(1)}, f32[2688]{0:T(1024)}, u32[]{:S(2)}) copy-start(f32[2688]{0:T(1024)} %param.35) | copy-start | bytes 32260
  534.8 3.7 copy-start.19
  534.8 128.8 %all-to-all-start.2 = ((bf16[32,28,2688]{2,1,0:T(8,128)(2,1)}), bf16[32,28,2688]{2,1,0:T(8,128)(2,1)}, u32[]{:S(2)}, u32[]{:S(2)}) async-start(bf16[32,28,2688]{2,1,0:T(8,128)(2,1)} %copy.89), calls=%async_computation.3 | async-start | bytes 11010048 | tf_op jit(solution)/shard_map/all_to_all | solution.py:208
  690.0 4.3 copy-start.7
  690.0 5.5 copy-start.1
  (6 other events, 6.6 us)
Sparse Core Ops, SparseCore 0:
  10.4 92.1 all-gather.4
  160.6 15.3 all-gather.6
  227.3 107.2 reduce-scatter.1
where the time goes:
time: 710 us; the launch traced here: 702 us
  waiting for transfers between devices  306 us (43%)
  blocking collectives  135 us (19%)
  local copies, waits for them, and re-layouts  107 us (15%)
  matrix products  83 us (12%)
  other arithmetic  43.4 us (6%)
  between operations  14.3 us (2%)
  starting transfers between devices  13.1 us (2%)
    all_to_all x1, blocking collectives, shards(): lax.all_to_all(outgoing, ('ctx', 'wide'), split_axis=0, concat_axis=0, ti...  128 us
    all_to_all x1, waiting for transfers between devices, shards(): lax.all_to_all(expert_apply(lax.all_to_all(outgoing, ('ctx', 'wide'), spl...  125 us
    reduce_scatter x1, waiting for transfers between devices, shards(): lax.psum_scatter(jnp.dot(gated, w_out, preferred_element_type=jnp.float32...  104 us
    all_gather x1, waiting for transfers between devices, shards(): lax.all_gather(normed, 'wide', axis=0, tiled=True)  71.1 us
    dot_general x1, matrix products, expert_apply(): jnp.einsum('secf,efd->secd', activated, w_down, preferred_element_type=jn...  33.2 us
    reshape x2, local copies, waits for them, and re-layouts, shards(): returned.reshape(experts * capacity, model_width)[slot_index]  14.6 us
  transfers between devices with their start and end apart: 6, of which 4 were waited for; matrix products, arithmetic and copies ran while one was open for 6% of the time, Pallas kernels for 0%

commit v1 on v0

v1 whole, which is shorter than its diff:
```python
import functools

import jax
import jax.numpy as jnp
from jax import lax
from jax.experimental import pallas as pl
from jax.experimental.pallas import tpu as pltpu
from jax.sharding import PartitionSpec as P

STATE = 128
GROUPS = 8
KERNEL = 4
TOP = 6
RIM = 8

EPSILON = 1e-05
PRECISE = lax.Precision.HIGHEST
VMEM_BYTES = 48 * 1024 * 1024


def ring_of(count):
    columns = 1
    while columns * columns * 4 <= count:
        columns *= 2
    rows = count // columns
    if columns == 1 or rows % 2:
        return list(range(count))
    walk = [row * columns for row in range(rows)]
    for lap, row in enumerate(reversed(range(rows))):
        line = list(range(1, columns))
        if lap % 2:
            line.reverse()
        walk += [row * columns + column for column in line]
    return walk


class Ring:
    def __init__(self, count):
        self.count = count
        self.half = count // 2
        self.walk = ring_of(count)
        place = [0] * count
        for spot, index in enumerate(self.walk):
            place[index] = spot
        following = [(self.walk[i], self.walk[(i + 1) % count]) for i in range(count)]
        self.routes = {1: following, -1: [(b, a) for a, b in following]}
        here = jnp.asarray(place, jnp.int32)[lax.axis_index("wide")]
        self.groups = [[0]] + [[s, -s] for s in range(1, self.half)] + [[self.half]]
        flat = jnp.asarray([o for group in self.groups for o in group], jnp.int32)
        self.order = jnp.asarray(self.walk, jnp.int32)[(here + flat + count) % count]

    def send(self, block, way):
        return lax.ppermute(block, "wide", self.routes[way])

    def gather(self, block):
        yield block
        ahead = behind = block
        for _ in range(1, self.half):
            behind = self.send(behind, 1)
            ahead = self.send(ahead, -1)
            yield jnp.concatenate([ahead, behind], 0)
        cut = block.shape[0] // 2
        yield jnp.concatenate([self.send(behind[:cut], 1), self.send(ahead[cut:], -1)], 0)

    def scatter_sum(self, parts):
        rows = parts[0].shape[0]
        cut = rows // 2
        far = parts[self.half]
        up, down = self.send(far[:cut], 1), self.send(far[cut:], -1)
        for s in range(self.half - 1, 0, -1):
            ahead, behind = parts[s][:rows], parts[s][rows:]
            if s == self.half - 1:
                none = jnp.zeros_like(up)
                up = jnp.concatenate([up, none], 0)
                down = jnp.concatenate([none, down], 0)
            up = self.send((ahead.astype(jnp.float32) + up.astype(jnp.float32)).astype(far.dtype), 1)
            down = self.send((behind.astype(jnp.float32) + down.astype(jnp.float32)).astype(far.dtype), -1)
        return parts[0].astype(jnp.float32) + up.astype(jnp.float32) + down.astype(jnp.float32)


def partner_2(block, axis, bit):
    count = lax.axis_size(axis)
    route = []
    for low in range(count):
        high = low | 1 << bit
        if high != low and high < count:
            route += [(low, high), (high, low)]
    return lax.ppermute(block, axis, route)


def shifted(block, axis, distance):
    devices = range(lax.axis_size(axis))
    route = [(i - distance, i) for i in devices if i - distance in devices]
    return lax.ppermute(block, axis, route)


def doubled_gather(block, axis):
    index = lax.axis_index(axis)
    for bit_number in range(lax.axis_size(axis).bit_length() - 1):
        other = partner_2(block, axis, bit_number)
        upper = index // 2**bit_number % 2 == 1
        block = jnp.where(
            upper, jnp.concatenate([other, block], 0), jnp.concatenate([block, other], 0)
        )
    return block


def last_of(block, axis):
    index = lax.axis_index(axis)
    for bit_number in range(lax.axis_size(axis).bit_length() - 1):
        other = partner_2(block, axis, bit_number)
        block = jnp.where(index // 2**bit_number % 2 == 1, block, other)
    return block


def rms_scale(values, gain_vec):
    mean_sq = jnp.mean(values * values, axis=-1, keepdims=True)
    return values * lax.rsqrt(mean_sq + EPSILON) * gain_vec


def spread(values, fan):
    high = values.astype(jnp.bfloat16)
    low = (values - high.astype(jnp.float32)).astype(jnp.bfloat16)
    return jnp.dot(high, fan, preferred_element_type=jnp.float32) + jnp.dot(
        low, fan, preferred_element_type=jnp.float32
    )


def softplus(values):
    return jnp.maximum(values, 0.0) + jnp.log1p(jnp.exp(-jnp.abs(values)))


def silu(values):
    return values / (1.0 + jnp.exp(-values))


def conv_silu(current, before, taps):
    rows = current.shape[0]
    extended = jnp.concatenate([before, current], 0)
    first = RIM - (KERNEL - 1)
    total = taps[0:1] * extended[first : first + rows]
    for offset in range(1, KERNEL):
        total = total + taps[offset : offset + 1] * extended[first + offset : first + offset + rows]
    return silu(total)


def ssd_kernel(groups, refs):
    count = sum(groups)
    order = refs[0]
    pieces = len(groups)
    x_in, bc_in, dt_in, dtt_in = (refs[1 + k * pieces : 1 + (k + 1) * pieces] for k in range(4))
    (
        rim_x, rim_bc, bias_row, bias_col, rate_row, rate_col, taps_x, taps_bc, skip_row, fan,
        y_out, c_out, cum_out, state_out,
        xs, bcs, dts, dtts, before_x, before_bc, state, passed, arrivals,
    ) = refs[1 + 4 * pieces :]
    rows = xs.shape[1]
    heads = bias_row.shape[1]
    width = xs.shape[2]
    head_dim = width // heads
    copies = []
    spot = 0
    for g, size in enumerate(groups):
        for j in range(size):
            seq = order[spot]
            span = pl.ds(j * rows, rows)
            moves = [
                (x_in[g].at[span], xs.at[seq]),
                (bc_in[g].at[span], bcs.at[seq]),
                (dt_in[g].at[span], dts.at[seq]),
                (dtt_in[g].at[:, span], dtts.at[seq]),
            ]
            for k, (source, target) in enumerate(moves):
                copies.append(pltpu.make_async_copy(source, target, arrivals.at[k, spot]))
                copies[-1].start()
            spot += 1
    for copy in copies:
        copy.wait()
    before_x[...] = rim_x[...].astype(jnp.float32)
    before_bc[...] = rim_bc[...].astype(jnp.float32)
    state[...] = jnp.zeros_like(state)
    passed[...] = jnp.zeros_like(passed)
    row_id = lax.broadcasted_iota(jnp.int32, (rows, rows), 0)
    col_id = lax.broadcasted_iota(jnp.int32, (rows, rows), 1)
    causal = row_id >= col_id
    lower = jnp.where(causal, 1.0, 0.0).astype(jnp.float32)
    upper = jnp.where(row_id <= col_id, 1.0, 0.0).astype(jnp.float32)
    pair = 2 * head_dim
    left = lax.broadcasted_iota(jnp.int32, (rows, pair), 1) < head_dim

    def one(i, carry):
        x_now = xs[i].astype(jnp.float32)
        bc_now = bcs[i].astype(jnp.float32)
        x = conv_silu(x_now, before_x[...], taps_x[...])
        bc = conv_silu(bc_now, before_bc[...], taps_bc[...])
        before_x[...] = x_now[rows - RIM :]
        before_bc[...] = bc_now[rows - RIM :]
        b = bc[:, :STATE]
        c = bc[:, STATE:].astype(jnp.bfloat16)
        b_t = jnp.transpose(b).astype(jnp.bfloat16)
        dt = softplus(dts[i] + bias_row[...])
        dt_t = softplus(dtts[i] + bias_col[...])
        cum = jnp.dot(lower, dt * rate_row[...], precision=PRECISE, preferred_element_type=jnp.float32)
        cum_t = jnp.dot(dt_t * rate_col[...], upper, precision=PRECISE, preferred_element_type=jnp.float32)
        last = cum[rows - 1 : rows]
        scores = jnp.dot(c, b_t, preferred_element_type=jnp.float32)
        x_dt = x * spread(dt, fan[...])
        x_low = x_dt.astype(jnp.bfloat16)
        earlier = jnp.dot(c, state[...].astype(jnp.bfloat16), preferred_element_type=jnp.float32)
        rest = spread(jnp.exp(cum), fan[...]) * earlier + skip_row[...] * x
        for h in range(0, heads, 2):
            weights = []
            for k in (h, h + 1):
                gap = cum[:, k : k + 1] - cum_t[k : k + 1, :]
                weights.append((scores * jnp.exp(jnp.where(causal, gap, -1e30))).astype(jnp.bfloat16))
            units = slice(h * head_dim, h * head_dim + pair)
            both = x_low[:, units]
            none = jnp.zeros_like(both)
            stacked = jnp.concatenate([jnp.where(left, both, none), jnp.where(left, none, both)], 0)
            y = jnp.dot(jnp.concatenate(weights, 1), stacked, preferred_element_type=jnp.float32)
            y_out[i, :, units] = y + rest[:, units]
        tail = (x_dt * spread(jnp.exp(last - cum), fan[...])).astype(jnp.bfloat16)
        grown = jnp.dot(b_t, tail, preferred_element_type=jnp.float32)
        c_out[i] = c
        cum_out[i] = cum + passed[...]
        passed[...] = passed[...] + last
        fade = spread(jnp.broadcast_to(jnp.exp(last), (8, heads)), fan[...])
        state[...] = fade[0:1] * state[...] + grown
        return carry

    lax.fori_loop(0, count, one, 0)
    state_out[:STATE] = state[...]
    state_out[STATE:] = spread(jnp.broadcast_to(passed[...], (8, heads)), fan[...])


def gate_kernel(groups, refs):
    order, y_in, c_in, cum_in, state_in, gain_row, fan, gather = refs[:8]
    gates = refs[8 : 8 + len(groups)]
    outs = refs[8 + len(groups) :]
    rows = y_in.shape[1]
    head_dim = y_in.shape[2] // cum_in.shape[2]
    incoming = state_in[...].astype(jnp.bfloat16)
    spot = 0
    for g, size in enumerate(groups):
        for j in range(size):
            seq = order[spot]
            span = slice(j * rows, (j + 1) * rows)
            earlier = jnp.dot(c_in[seq], incoming, preferred_element_type=jnp.float32)
            y = y_in[seq] + spread(jnp.exp(cum_in[seq]), fan[...]) * earlier
            gated = y * silu(gates[g][span].astype(jnp.float32))
            squares = jnp.dot(
                (gated * gated).astype(jnp.bfloat16), gather[...], preferred_element_type=jnp.float32
            )
            scale = lax.rsqrt(squares / head_dim + EPSILON)
            outs[g][span] = (gated * spread(scale, fan[...]) * gain_row[...]).astype(jnp.bfloat16)
            spot += 1


def vmem(count):
    return [pl.BlockSpec(memory_space=pltpu.VMEM)] * count


def call(kernel, ins, outs, scratch, flops, far=0):
    moved = sum(a.size * a.dtype.itemsize for a in list(ins) + list(outs))
    return pl.pallas_call(
        lambda *refs: kernel(refs),
        out_shape=outs,
        in_specs=[pl.BlockSpec(memory_space=pltpu.SMEM)]
        + [pl.BlockSpec(memory_space=pl.ANY)] * far
        + vmem(len(ins) - 1 - far),
        out_specs=vmem(len(outs)),
        scratch_shapes=scratch,
        compiler_params=pltpu.CompilerParams(vmem_limit_bytes=VMEM_BYTES),
        cost_estimate=pl.CostEstimate(flops=flops, bytes_accessed=moved, transcendentals=0),
    )(*ins)


def shards(
    tokens,
    mamba_gain,
    w_z,
    w_x,
    w_bc,
    w_dt,
    dt_bias,
    a_log,
    conv_x,
    conv_bc,
    skip,
    norm_gain,
    w_out,
    moe_gain,
    expert_ids,
    router_weights,
    w_up,
    w_down,
):
    wide_count = lax.axis_size("wide")
    ctx_count = lax.axis_size("ctx")
    tok_rows, model_width = tokens.shape
    heads_here = dt_bias.shape[0]
    inner_here = w_z.shape[1]
    head_dim = inner_here // heads_here
    position = lax.axis_index("wide")
    ctx_index = lax.axis_index("ctx")
    ring = Ring(wide_count)
    sizes = [len(group) for group in ring.groups]
    bf16, f32 = jnp.bfloat16, jnp.float32

    stream = tokens.astype(f32)
    normed = rms_scale(stream, mamba_gain).astype(bf16)

    choices = jnp.concatenate([expert_ids.astype(f32), router_weights], 1)
    span_choices = doubled_gather(choices, "wide").reshape(wide_count, tok_rows, 2 * TOP)[ring.order]
    experts = ctx_count * wide_count
    capacity = max(2, (7 * tok_rows * TOP + 6 * experts - 1) // (6 * experts))
    peers = (ctx_index ^ jnp.arange(ctx_count, dtype=jnp.int32)) * wide_count + position
    picks, weighings = [], []
    start = 0
    for size in sizes:
        part = span_choices[start : start + size].reshape(size * tok_rows, 2 * TOP)
        start += size
        chosen = part[:, :TOP].astype(jnp.int32)
        named = chosen[None] == peers[:, None, None]
        member = jnp.any(named, axis=2)
        weight = jnp.sum(jnp.where(named, part[None, :, TOP:], 0.0), axis=2)
        counted = member.astype(jnp.int32)
        rank = jnp.cumsum(counted, axis=1) - counted
        slots = jnp.arange(size * capacity, dtype=jnp.int32)
        here = member[:, None, :] & (rank[:, None, :] == slots[None, :, None])
        picks.append(here.astype(bf16).reshape(-1, size * tok_rows))
        weighings.append(
            jnp.where(here, weight[:, None, :], 0.0).astype(bf16).reshape(-1, size * tok_rows)
        )

    w_steps = lax.dynamic_slice_in_dim(w_dt, position * heads_here, heads_here, 1)
    members = wide_count // GROUPS

    def whole_bc(share):
        for bit_number in range(members.bit_length() - 1):
            partner = partner_2(share, "wide", bit_number)
            upper_half = position // 2**bit_number % 2
            share = jnp.where(
                upper_half == 1,
                jnp.concatenate([partner, share], 1),
                jnp.concatenate([share, partner], 1),
            )
        return share

    def project(rows, weight):
        return jnp.dot(rows, weight, preferred_element_type=f32)

    rim = last_of(shifted(normed[-RIM:], "ctx", 1), "wide")
    rim_x = project(rim, w_x).astype(bf16)
    rim_bc = whole_bc(project(rim, w_bc).astype(bf16))
    gates, x_ins, bc_ins, steps = [], [], [], []
    for rows in ring.gather(normed):
        gates.append(project(rows, w_z).astype(bf16))
        x_ins.append(project(rows, w_x).astype(bf16))
        bc_ins.append(whole_bc(project(rows, w_bc).astype(bf16)))
        steps.append(project(rows, w_steps))

    group_index = position // members
    taps_bc = lax.dynamic_slice_in_dim(conv_bc, group_index * 2 * STATE, 2 * STATE, 1)
    fan = jnp.repeat(jnp.eye(heads_here, dtype=bf16), head_dim, axis=1)
    rate = -jnp.exp(a_log)
    shape = jax.ShapeDtypeStruct
    y_local, c_all, cum_all, own_state = call(
        functools.partial(ssd_kernel, sizes),
        [ring.order, *x_ins, *bc_ins, *steps, *(jnp.transpose(s) for s in steps), rim_x, rim_bc]
        + [dt_bias[None], dt_bias[:, None], rate[None], rate[:, None], conv_x, taps_bc]
        + [jnp.repeat(skip, head_dim)[None], fan],
        [
            shape((wide_count, tok_rows, inner_here), f32),
            shape((wide_count, tok_rows, STATE), bf16),
            shape((wide_count, tok_rows, heads_here), f32),
            shape((STATE + 8, inner_here), f32),
        ],
        [
            pltpu.VMEM((wide_count, tok_rows, inner_here), bf16),
            pltpu.VMEM((wide_count, tok_rows, 2 * STATE), bf16),
            pltpu.VMEM((wide_count, tok_rows, heads_here), f32),
            pltpu.VMEM((wide_count, heads_here, tok_rows), f32),
            pltpu.VMEM((RIM, inner_here), f32),
            pltpu.VMEM((RIM, 2 * STATE), f32),
            pltpu.VMEM((STATE, inner_here), f32),
            pltpu.VMEM((1, heads_here), f32),
            pltpu.SemaphoreType.DMA((4, wide_count)),
        ],
        wide_count * 8 * tok_rows * tok_rows * inner_here,
        4 * len(sizes),
    )

    def join(earlier, later):
        return (
            earlier[0] + later[0],
            jnp.exp(later[0]) * earlier[1] + later[1],
        )

    total = (own_state[STATE : STATE + 1], own_state[:STATE])
    prior = (jnp.zeros_like(total[0]), jnp.zeros_like(total[1]))
    for bit_number in range(ctx_count.bit_length() - 1):
        sent = jnp.concatenate([total[1], jnp.broadcast_to(total[0], (8, inner_here))], 0)
        other = partner_2(sent, "ctx", bit_number)
        other = (other[STATE : STATE + 1], other[:STATE])
        upper = ctx_index // 2**bit_number % 2 == 1
        longer = join(other, prior)
        prior = jax.tree.map(lambda a, b: jnp.where(upper, a, b), longer, prior)
        if bit_number + 2 < ctx_count.bit_length():
            total = jax.tree.map(
                lambda a, b: jnp.where(upper, a, b), join(other, total), join(total, other)
            )

    gated = call(
        functools.partial(gate_kernel, sizes),
        [ring.order, y_local, c_all, cum_all, prior[1], norm_gain[None], fan, fan.T, *gates],
        [shape((size * tok_rows, inner_here), bf16) for size in sizes],
        [],
        wide_count * 8 * tok_rows * STATE * inner_here,
    )
    shares = [None] * len(sizes)
    for g in reversed(range(len(sizes))):
        shares[g] = lax.optimization_barrier(project(gated[g], w_out).astype(bf16))
    mamba_out = ring.scatter_sum(shares)
    hidden_stream = (stream + mamba_out).astype(bf16)
    hidden_f32 = hidden_stream.astype(f32)
    moe_in = rms_scale(hidden_f32, moe_gain).astype(bf16)

    def swap(block, distance):
        if distance == 0:
            return block
        route = [(i, i ^ distance) for i in range(ctx_count)]
        return lax.ppermute(block, "ctx", route)

    def cross(rows, size):
        deep = size * capacity
        return jnp.concatenate(
            [swap(rows[d * deep : (d + 1) * deep], d) for d in range(ctx_count)], 0
        )

    results = []
    for g, rows in enumerate(ring.gather(moe_in)):
        picked = project(picks[g], rows).astype(bf16)
        arrived = cross(picked, sizes[g])
        activated = jax.nn.relu(project(arrived, w_up[0]))
        activated = (activated * activated).astype(bf16)
        expert_out = project(activated, w_down[0]).astype(bf16)
        returned = cross(expert_out, sizes[g])
        results.append(
            lax.optimization_barrier(
                lax.dot_general(
                    weighings[g], returned, (((0,), (0,)), ((), ())), preferred_element_type=f32
                ).astype(bf16)
            )
        )
    return (hidden_f32 + ring.scatter_sum(results)).astype(bf16)


def solution(mesh):
    placed = (
        P(("ctx", "wide"), None),
        P(),
        P(None, "wide"),
        P(None, "wide"),
        P(None, "wide"),
        P(),
        P("wide"),
        P("wide"),
        P(None, "wide"),
        P(),
        P("wide"),
        P("wide"),
        P("wide", None),
        P(),
        P(("ctx", "wide"), None),
        P(("ctx", "wide"), None),
        P(("ctx", "wide"), None, None),
        P(("ctx", "wide"), None, None),
    )
    return jax.shard_map(
        shards, mesh=mesh, in_specs=placed, out_specs=P(("ctx", "wide"), None), check_vma=False
    )
```

time: 710 us -> 445 us (0.63)
  waiting for transfers between devices: 306 us -> 142 us
  blocking collectives: 135 us -> 0 us
  starting transfers between devices: 13.1 us -> 69.9 us
  local copies, waits for them, and re-layouts: 107 us -> 57.5 us
  matrix products: 83 us -> 119 us
  Pallas kernels: 0 us -> 17.9 us
  other arithmetic: 43.4 us -> 29 us
  between operations: 14.3 us -> 1.88 us
    ppermute x0 -> x70, waiting for transfers between devices: none -> 142 us  [the longest x32 88.1 us: send(): return lax.ppermute(block, 'wide', self.routes[way])]
    all_to_all x2 -> x0, waiting for transfers between devices: 130 us -> none  [the longest x1 125 us: shards(): lax.all_to_all(expert_apply(lax.all_to_all(outgoing, ('ctx', 'wide'), spl...]
    all_to_all x1 -> x0, blocking collectives: 128 us -> none  [shards(): lax.all_to_all(outgoing, ('ctx', 'wide'), split_axis=0, concat_axis=0, ti...]
    reduce_scatter x1 -> x0, waiting for transfers between devices: 104 us -> none  [shards(): lax.psum_scatter(jnp.dot(gated, w_out, preferred_element_type=jnp.float32...]
    all_gather x2 -> x0, waiting for transfers between devices: 71.1 us -> none  [the longest x1 71.1 us: shards(): lax.all_gather(normed, 'wide', axis=0, tiled=True)]
    ppermute x0 -> x70, starting transfers between devices: none -> 68.6 us  [the longest x32 35.3 us: send(): return lax.ppermute(block, 'wide', self.routes[way])]
    reshape x6 -> x2, local copies, waits for them, and re-layouts: 37.8 us -> 0.08 us  [the longest x1 0.07 us: shards(): fan = jnp.repeat(jnp.eye(heads_here, dtype=bf16), head_dim, axis=1)]
    dot_general x9 -> x42, matrix products: 83 us -> 119 us  [the longest x37 114 us: project(): return jnp.dot(rows, weight, preferred_element_type=f32)]
  transfers between devices with their start and end apart: 6 -> 71, of which waited for: 4 -> 38; matrix products, arithmetic and copies ran while one was open for 6% -> 33% of each run, Pallas kernels for 0% -> 0%
where the time goes in v1:
time: 445 us; the launch traced here: 436 us
  waiting for transfers between devices  142 us (32%)
  matrix products  119 us (27%)
  starting transfers between devices  69.9 us (16%)
  local copies, waits for them, and re-layouts  57.5 us (13%)
  other arithmetic  29 us (7%)
  Pallas kernels  17.9 us (4%)
    dot_general x37, matrix products, project(): return jnp.dot(rows, weight, preferred_element_type=f32)  114 us
    ppermute x32, waiting for transfers between devices, send(): return lax.ppermute(block, 'wide', self.routes[way])  88.1 us
    ppermute x30, waiting for transfers between devices, swap(): return lax.ppermute(block, 'ctx', route)  35.9 us
    ppermute x32, starting transfers between devices, send(): return lax.ppermute(block, 'wide', self.routes[way])  35.3 us
    unnamed x242, local copies, waits for them, and re-layouts  30 us
    ppermute x30, starting transfers between devices, swap(): return lax.ppermute(block, 'ctx', route)  21.5 us
    pallas_call x2, Pallas kernels, call(): pl.pallas_call(lambda *refs: kernel(refs), out_shape=outs, in_specs=[pl.B...  17.9 us
    ppermute x8, waiting for transfers between devices, partner_2(): return lax.ppermute(block, axis, route)  17.4 us
  transfers between devices with their start and end apart: 71, of which 38 were waited for; matrix products, arithmetic and copies ran while one was open for 33% of the time, Pallas kernels for 0%

profile of v1, /device:TPU:0, one launch (start us, length us, event | category | flops | bytes accessed | tf_op | source)
XLA Modules:
  0.0 436.5 jit_solution(4074998272972740548)
XLA Ops:
  67.1 3.8 convolution_convert_fusion.17.refs_9_
  72.5 5.3 %collective-permute-done.2 = bf16[128,2688]{1,0:T(8,128)(2,1)} collective-permute-done((bf16[128,2688]{1,0:T(8,128)(2,1)}, bf16[128,2688]{1,0:T(8,128)(2,1)}, u32[]{:S(2)}, u32[]{:S(2)}) %collective-permute-start.2) | collective-permute-done | bytes 688160 | tf_op jit(solution)/shard_map/ppermute | solution.py:53
  85.8 4.0 convolution_convert_fusion.16.refs_10_
  91.4 5.0 %collective-permute-done.5 = bf16[128,2688]{1,0:T(8,128)(2,1)} collective-permute-done((bf16[128,2688]{1,0:T(8,128)(2,1)}, bf16[128,2688]{1,0:T(8,128)(2,1)}, u32[]{:S(2)}, u32[]{:S(2)}) %collective-permute-start.5) | collective-permute-done | bytes 688160 | tf_op jit(solution)/shard_map/ppermute | solution.py:53
  138.2 13.7 %shard_map.199 = (f32[8,128,512]{2,1,0:T(8,128)S(1)}, bf16[8,128,128]{2,1,0:T(8,128)(2,1)S(1)}, f32[8,128,8]{2,1,0:T(8,128)S(1)}, f32[136,512]{1,0:T(8,128)S(1)}) custom-call(s32[8]{0:T(128)S(1)} %copy-done.33, bf16[128,512]{1,0:T(8,128)(2,1)S(1)} %convolution_convert_fusion.27.refs_1_, bf16[256,512]{1,0:T(8,128)(2,1)S(1)} %copy-done.6, ...), custom_call_target="tpu_custom_call" | custom-call | flops 536870912 | bytes 4343968 | tf_op jit(solution)/shard_map/pallas_call | solution.py:265
  157.1 6.8 %collective-permute-done.13 = f32[136,512]{1,0:T(8,128)S(1)} collective-permute-done((f32[136,512]{1,0:T(8,128)S(1)}, f32[136,512]{1,0:T(8,128)S(1)}, u32[]{:S(2)}, u32[]{:S(2)}) %collective-permute-start.13) | collective-permute-done | bytes 278560 | tf_op jit(solution)/shard_map/ppermute | solution.py:88
  163.9 4.1 shard_map.200
  175.9 3.9 collective-permute-done.14
  185.7 12.8 %collective-permute-done.15 = bf16[128,2688]{1,0:T(8,128)(2,1)S(1)} collective-permute-done((bf16[128,2688]{1,0:T(8,128)(2,1)S(1)}, bf16[128,2688]{1,0:T(8,128)(2,1)S(1)}, u32[]{:S(2)}, u32[]{:S(2)}) %collective-permute-start.15) | collective-permute-done | bytes 688160 | tf_op jit(solution)/shard_map/ppermute | solution.py:53
  202.3 11.7 %collective-permute-done.16 = bf16[128,2688]{1,0:T(8,128)(2,1)S(1)} collective-permute-done((bf16[128,2688]{1,0:T(8,128)(2,1)S(1)}, bf16[128,2688]{1,0:T(8,128)(2,1)S(1)}, u32[]{:S(2)}, u32[]{:S(2)}) %collective-permute-start.16) | collective-permute-done | bytes 688160 | tf_op jit(solution)/shard_map/ppermute | solution.py:53
  223.7 7.2 %collective-permute-done.17 = bf16[128,2688]{1,0:T(8,128)(2,1)} collective-permute-done((bf16[128,2688]{1,0:T(8,128)(2,1)}, bf16[128,2688]{1,0:T(8,128)(2,1)}, u32[]{:S(2)}, u32[]{:S(2)}) %collective-permute-start.17) | collective-permute-done | bytes 688160 | tf_op jit(solution)/shard_map/ppermute | solution.py:53
  237.2 12.3 %collective-permute-done.32 = bf16[128,2688]{1,0:T(8,128)(2,1)S(1)} collective-permute-done((bf16[128,2688]{1,0:T(8,128)(2,1)S(1)}, bf16[128,2688]{1,0:T(8,128)(2,1)S(1)}, u32[]{:S(2)}, u32[]{:S(2)}) %collective-permute-start.32) | collective-permute-done | bytes 688160 | tf_op jit(solution)/shard_map/ppermute | solution.py:53
  254.1 7.2 %collective-permute-done.40 = bf16[128,2688]{1,0:T(8,128)(2,1)S(1)} collective-permute-done((bf16[128,2688]{1,0:T(8,128)(2,1)S(1)}, bf16[128,2688]{1,0:T(8,128)(2,1)S(1)}, u32[]{:S(2)}, u32[]{:S(2)}) %collective-permute-start.40) | collective-permute-done | bytes 688160 | tf_op jit(solution)/shard_map/ppermute | solution.py:53
  268.7 12.9 %fusion.20 = bf16[224,2688]{1,0:T(8,128)(2,1)S(1)} fusion(bf16[1,1856,2688]{2,1,0:T(8,128)(2,1)} %param.38, bf16[1,2688,1856]{1,2,0:T(8,128)(2,1)} %param.37, bf16[56,2688]{1,0:T(8,128)(2,1)} %copy-done.104, bf16[56,2688]{1,0:T(8,128)(2,1)} %copy-done.106, bf16[56,2688]{1,0:T(8,128)(2,1)} %copy-done.108, bf16[56,2688]{1,0:T(8,128)(2,1)S(1)} %get-tuple-element.51), kind=kOutput, calls=%fused_computation.28 | convolution fusion | flops 4476745728 | bytes 22364160 | tf_op jit(solution)/shard_map/dot_general | solution.py:351
  283.6 13.9 %fusion.23 = bf16[224,2688]{1,0:T(8,128)(2,1)} fusion(bf16[1,1856,2688]{2,1,0:T(8,128)(2,1)} %param.38, bf16[1,2688,1856]{1,2,0:T(8,128)(2,1)} %param.37, bf16[56,2688]{1,0:T(8,128)(2,1)} %collective-permute-done.43, bf16[56,2688]{1,0:T(8,128)(2,1)} %collective-permute-done.42, bf16[56,2688]{1,0:T(8,128)(2,1)} %collective-permute-done.41, ...), kind=kOutput, calls=%fused_computation.29 | convolution fusion | flops 4476745728 | bytes 22364160 | tf_op jit(solution)/shard_map/dot_general | solution.py:351
  315.7 5.7 %collective-permute-done.50 = bf16[56,2688]{1,0:T(8,128)(2,1)S(1)} collective-permute-done((bf16[56,2688]{1,0:T(8,128)(2,1)S(1)}, bf16[56,2688]{1,0:T(8,128)(2,1)S(1)}, u32[]{:S(2)}, u32[]{:S(2)}) %collective-permute-start.50) | collective-permute-done | bytes 301088 | tf_op jit(solution)/shard_map/ppermute | solution.py:433
  322.8 13.9 %fusion.26 = bf16[224,2688]{1,0:T(8,128)(2,1)} fusion(bf16[1,1856,2688]{2,1,0:T(8,128)(2,1)} %param.38, bf16[1,2688,1856]{1,2,0:T(8,128)(2,1)} %param.37, bf16[56,2688]{1,0:T(8,128)(2,1)} %copy-done.103, bf16[56,2688]{1,0:T(8,128)(2,1)} %copy-done.105, bf16[56,2688]{1,0:T(8,128)(2,1)} %copy-done.107, bf16[56,2688]{1,0:T(8,128)(2,1)S(1)} %get-tuple-element.67), kind=kOutput, calls=%fused_computation.30 | convolution fusion | flops 4476745728 | bytes 22364160 | tf_op jit(solution)/shard_map/dot_general | solution.py:351
  336.7 11.7 %fusion.32 = bf16[112,2688]{1,0:T(8,128)(2,1)S(1)} fusion(bf16[1,1856,2688]{2,1,0:T(8,128)(2,1)} %param.38, bf16[1,2688,1856]{1,2,0:T(8,128)(2,1)} %param.37, bf16[28,2688]{1,0:T(8,128)(2,1)S(1)} %collective-permute-done.59, bf16[28,2688]{1,0:T(8,128)(2,1)S(1)} %collective-permute-done.58, bf16[28,2688]{1,0:T(8,128)(2,1)} %collective-permute-done.57, ...), kind=kOutput, calls=%fused_computation.39 | convolution fusion | flops 2238372864 | bytes 21159936 | tf_op jit(solution)/shard_map/dot_general | solution.py:351
  355.8 3.9 collective-permute-done.61
  366.8 5.8 %collective-permute-done.53 = bf16[56,2688]{1,0:T(8,128)(2,1)S(1)} collective-permute-done((bf16[56,2688]{1,0:T(8,128)(2,1)S(1)}, bf16[56,2688]{1,0:T(8,128)(2,1)S(1)}, u32[]{:S(2)}, u32[]{:S(2)}) %collective-permute-start.53) | collective-permute-done | bytes 301088 | tf_op jit(solution)/shard_map/ppermute | solution.py:433
  379.7 5.8 %collective-permute-done.45 = bf16[56,2688]{1,0:T(8,128)(2,1)S(1)} collective-permute-done((bf16[56,2688]{1,0:T(8,128)(2,1)S(1)}, bf16[56,2688]{1,0:T(8,128)(2,1)S(1)}, u32[]{:S(2)}, u32[]{:S(2)}) %collective-permute-start.45) | collective-permute-done | bytes 301088 | tf_op jit(solution)/shard_map/ppermute | solution.py:433
  387.1 5.2 %collective-permute-done.64 = bf16[128,2688]{1,0:T(8,128)(2,1)S(1)} collective-permute-done((bf16[128,2688]{1,0:T(8,128)(2,1)S(1)}, bf16[128,2688]{1,0:T(8,128)(2,1)S(1)}, u32[]{:S(2)}, u32[]{:S(2)}) %collective-permute-start.64) | collective-permute-done | bytes 688160 | tf_op jit(solution)/shard_map/ppermute | solution.py:53
  397.3 11.6 %fusion.29 = bf16[112,2688]{1,0:T(8,128)(2,1)S(1)} fusion(bf16[1,1856,2688]{2,1,0:T(8,128)(2,1)} %param.38, bf16[1,2688,1856]{1,2,0:T(8,128)(2,1)} %param.37, bf16[28,2688]{1,0:T(8,128)(2,1)S(1)} %collective-permute-done.27, bf16[28,2688]{1,0:T(8,128)(2,1)S(1)} %collective-permute-done.26, bf16[28,2688]{1,0:T(8,128)(2,1)S(1)} %collective-permute-done.25, ...), kind=kOutput, calls=%fused_computation.38 | convolution fusion | flops 2238372864 | bytes 21159936 | tf_op jit(solution)/shard_map/dot_general | solution.py:351
  420.8 4.7 %collective-permute-done.30 = bf16[28,2688]{1,0:T(8,128)(2,1)S(1)} collective-permute-done((bf16[28,2688]{1,0:T(8,128)(2,1)S(1)}, bf16[28,2688]{1,0:T(8,128)(2,1)S(1)}, u32[]{:S(2)}, u32[]{:S(2)}) %collective-permute-start.30) | collective-permute-done | bytes 150560 | tf_op jit(solution)/shard_map/ppermute | solution.py:433
  (544 shorter events, 241.6 us)
Async XLA Ops:
  3.7 57.0 %collective-permute-start.1 = (bf16[128,2688]{1,0:T(8,128)(2,1)}, bf16[128,2688]{1,0:T(8,128)(2,1)}, u32[]{:S(2)}, u32[]{:S(2)}) collective-permute-start(bf16[128,2688]{1,0:T(8,128)(2,1)} %fusion.82), channel_id=1, source_target_pairs={{0,2},{2,4},{4,6},{6,7},{7,5},{5,3},{3,1},{1,0},{8,10},{10,12},{12... | collective-permute-start | bytes 2064392 | tf_op jit(solution)/shard_map/ppermute | solution.py:53
  6.7 52.7 %collective-permute-start = (bf16[128,2688]{1,0:T(8,128)(2,1)}, bf16[128,2688]{1,0:T(8,128)(2,1)}, u32[]{:S(2)}, u32[]{:S(2)}) collective-permute-start(bf16[128,2688]{1,0:T(8,128)(2,1)} %fusion.82), channel_id=1, source_target_pairs={{2,0},{4,2},{6,4},{7,6},{5,7},{3,5},{1,3},{0,1},{10,8},{12,10},{14... | collective-permute-start | bytes 2064392 | tf_op jit(solution)/shard_map/ppermute | solution.py:53
  6.8 16.4 %collective-permute-start.22 = (f32[128,12]{0,1:T(8,128)S(1)}, f32[128,12]{0,1:T(8,128)S(1)}, u32[]{:S(2)}, u32[]{:S(2)}) collective-permute-start(f32[128,12]{0,1:T(8,128)S(1)} %pad_maximum_fusion.2), channel_id=1, source_target_pairs={{0,1},{1,0},{2,3},{3,2},{4,5},{5,4},{6,7},{7,6},{8,9},{9,8},{10,11... | collective-permute-start | bytes 18440 | tf_op jit(solution)/shard_map/ppermute | solution.py:88
  9.6 31.7 %collective-permute-start.8 = (bf16[8,2688]{1,0:T(8,128)(2,1)S(1)}, bf16[8,2688]{1,0:T(8,128)(2,1)S(1)}, u32[]{:S(2)}, u32[]{:S(2)}) collective-permute-start(bf16[8,2688]{1,0:T(8,128)(2,1)S(1)} %slice.354), channel_id=1, source_target_pairs={{0,8},{8,16},{16,24},{1,9},{9,17},{17,25},{2,10},{10,18},{18,26},{... | collective-permute-start | bytes 129032 | tf_op jit(solution)/shard_map/ppermute | solution.py:94
  182.6 15.9 %collective-permute-start.15 = (bf16[128,2688]{1,0:T(8,128)(2,1)S(1)}, bf16[128,2688]{1,0:T(8,128)(2,1)S(1)}, u32[]{:S(2)}, u32[]{:S(2)}) collective-permute-start(bf16[128,2688]{1,0:T(8,128)(2,1)S(1)} %get-tuple-element.45), channel_id=1, source_target_pairs={{0,2},{2,4},{4,6},{6,7},{7,5},{5,3},{3,1},{1,0},{8,10},{10,12},{12... | collective-permute-start | bytes 2064392 | tf_op jit(solution)/shard_map/ppermute | solution.py:53
  263.9 19.8 %collective-permute-start.43 = (bf16[56,2688]{1,0:T(8,128)(2,1)}, bf16[56,2688]{1,0:T(8,128)(2,1)}, u32[]{:S(2)}, u32[]{:S(2)}) collective-permute-start(bf16[56,2688]{1,0:T(8,128)(2,1)} %get-tuple-element.60), channel_id=1, source_target_pairs={{0,24},{8,16},{16,8},{24,0},{1,25},{9,17},{17,9},{25,1},{2,26},{10... | collective-permute-start | bytes 903176 | tf_op jit(solution)/shard_map/ppermute | solution.py:433
  263.9 19.8 %collective-permute-start.42 = (bf16[56,2688]{1,0:T(8,128)(2,1)}, bf16[56,2688]{1,0:T(8,128)(2,1)}, u32[]{:S(2)}, u32[]{:S(2)}) collective-permute-start(bf16[56,2688]{1,0:T(8,128)(2,1)} %get-tuple-element.61), channel_id=1, source_target_pairs={{0,16},{8,24},{16,0},{24,8},{1,17},{9,25},{17,1},{25,9},{2,18},{10... | collective-permute-start | bytes 903176 | tf_op jit(solution)/shard_map/ppermute | solution.py:433
  264.5 19.1 %collective-permute-start.41 = (bf16[56,2688]{1,0:T(8,128)(2,1)S(1)}, bf16[56,2688]{1,0:T(8,128)(2,1)}, u32[]{:S(2)}, u32[]{:S(2)}) collective-permute-start(bf16[56,2688]{1,0:T(8,128)(2,1)S(1)} %get-tuple-element.62), channel_id=1, source_target_pairs={{0,8},{8,0},{16,24},{24,16},{1,9},{9,1},{17,25},{25,17},{2,10},{10... | collective-permute-start | bytes 903176 | tf_op jit(solution)/shard_map/ppermute | solution.py:433
  281.5 18.4 %collective-permute-start.48 = (bf16[128,2688]{1,0:T(8,128)(2,1)}, bf16[128,2688]{1,0:T(8,128)(2,1)}, u32[]{:S(2)}, u32[]{:S(2)}) collective-permute-start(bf16[128,2688]{1,0:T(8,128)(2,1)} %copy-done.100), channel_id=1, source_target_pairs={{0,2},{2,4},{4,6},{6,7},{7,5},{5,3},{3,1},{1,0},{8,10},{10,12},{12... | collective-permute-start | bytes 2064392 | tf_op jit(solution)/shard_map/ppermute | solution.py:53
  282.2 19.6 %collective-permute-start.47 = (bf16[128,2688]{1,0:T(8,128)(2,1)}, bf16[128,2688]{1,0:T(8,128)(2,1)}, u32[]{:S(2)}, u32[]{:S(2)}) collective-permute-start(bf16[128,2688]{1,0:T(8,128)(2,1)} %copy-done.99), channel_id=1, source_target_pairs={{2,0},{4,2},{6,4},{7,6},{5,7},{3,5},{1,3},{0,1},{10,8},{12,10},{14... | collective-permute-start | bytes 2064392 | tf_op jit(solution)/shard_map/ppermute | solution.py:53
  313.2 23.5 %collective-permute-start.59 = (bf16[28,2688]{1,0:T(8,128)(2,1)S(1)}, bf16[28,2688]{1,0:T(8,128)(2,1)S(1)}, u32[]{:S(2)}, u32[]{:S(2)}) collective-permute-start(bf16[28,2688]{1,0:T(8,128)(2,1)S(1)} %get-tuple-element.88), channel_id=1, source_target_pairs={{0,24},{8,16},{16,8},{24,0},{1,25},{9,17},{17,9},{25,1},{2,26},{10... | collective-permute-start | bytes 451592 | tf_op jit(solution)/shard_map/ppermute | solution.py:433
  313.3 23.4 %collective-permute-start.58 = (bf16[28,2688]{1,0:T(8,128)(2,1)S(1)}, bf16[28,2688]{1,0:T(8,128)(2,1)S(1)}, u32[]{:S(2)}, u32[]{:S(2)}) collective-permute-start(bf16[28,2688]{1,0:T(8,128)(2,1)S(1)} %get-tuple-element.89), channel_id=1, source_target_pairs={{0,16},{8,24},{16,0},{24,8},{1,17},{9,25},{17,1},{25,9},{2,18},{10... | collective-permute-start | bytes 451592 | tf_op jit(solution)/shard_map/ppermute | solution.py:433
  315.7 21.0 %collective-permute-start.57 = (bf16[28,2688]{1,0:T(8,128)(2,1)S(1)}, bf16[28,2688]{1,0:T(8,128)(2,1)}, u32[]{:S(2)}, u32[]{:S(2)}) collective-permute-start(bf16[28,2688]{1,0:T(8,128)(2,1)S(1)} %get-tuple-element.90), channel_id=1, source_target_pairs={{0,8},{8,0},{16,24},{24,16},{1,9},{9,1},{17,25},{25,17},{2,10},{10... | collective-permute-start | bytes 451592 | tf_op jit(solution)/shard_map/ppermute | solution.py:433
  352.0 20.6 %collective-permute-start.53 = (bf16[56,2688]{1,0:T(8,128)(2,1)S(1)}, bf16[56,2688]{1,0:T(8,128)(2,1)S(1)}, u32[]{:S(2)}, u32[]{:S(2)}) collective-permute-start(bf16[56,2688]{1,0:T(8,128)(2,1)S(1)} %get-tuple-element.65), channel_id=1, source_target_pairs={{0,16},{8,24},{16,0},{24,8},{1,17},{9,25},{17,1},{25,9},{2,18},{10... | collective-permute-start | bytes 903176 | tf_op jit(solution)/shard_map/ppermute | solution.py:433
  354.5 19.0 %collective-permute-start.52 = (bf16[56,2688]{1,0:T(8,128)(2,1)S(1)}, bf16[56,2688]{1,0:T(8,128)(2,1)S(1)}, u32[]{:S(2)}, u32[]{:S(2)}) collective-permute-start(bf16[56,2688]{1,0:T(8,128)(2,1)S(1)} %get-tuple-element.66), channel_id=1, source_target_pairs={{0,8},{8,0},{16,24},{24,16},{1,9},{9,1},{17,25},{25,17},{2,10},{10... | collective-permute-start | bytes 903176 | tf_op jit(solution)/shard_map/ppermute | solution.py:433
  374.4 17.9 %collective-permute-start.64 = (bf16[128,2688]{1,0:T(8,128)(2,1)S(1)}, bf16[128,2688]{1,0:T(8,128)(2,1)S(1)}, u32[]{:S(2)}, u32[]{:S(2)}) collective-permute-start(bf16[128,2688]{1,0:T(8,128)(2,1)S(1)} %get-tuple-element.39), channel_id=1, source_target_pairs={{0,2},{2,4},{4,6},{6,7},{7,5},{5,3},{3,1},{1,0},{8,10},{10,12},{12... | collective-permute-start | bytes 2064392 | tf_op jit(solution)/shard_map/ppermute | solution.py:53
  375.2 17.8 %collective-permute-start.68 = (bf16[128,2688]{1,0:T(8,128)(2,1)S(1)}, bf16[128,2688]{1,0:T(8,128)(2,1)S(1)}, u32[]{:S(2)}, u32[]{:S(2)}) collective-permute-start(bf16[128,2688]{1,0:T(8,128)(2,1)S(1)} %get-tuple-element.40), channel_id=1, source_target_pairs={{2,0},{4,2},{6,4},{7,6},{5,7},{3,5},{1,3},{0,1},{10,8},{12,10},{14... | collective-permute-start | bytes 2064392 | tf_op jit(solution)/shard_map/ppermute | solution.py:53
  377.7 17.5 %collective-permute-start.27 = (bf16[28,2688]{1,0:T(8,128)(2,1)S(1)}, bf16[28,2688]{1,0:T(8,128)(2,1)S(1)}, u32[]{:S(2)}, u32[]{:S(2)}) collective-permute-start(bf16[28,2688]{1,0:T(8,128)(2,1)S(1)} %copy-done.61), channel_id=1, source_target_pairs={{0,24},{8,16},{16,8},{24,0},{1,25},{9,17},{17,9},{25,1},{2,26},{10... | collective-permute-start | bytes 451592 | tf_op jit(solution)/shard_map/ppermute | solution.py:433
  392.3 16.7 %collective-permute-start.38 = (bf16[56,2688]{1,0:T(8,128)(2,1)}, bf16[56,2688]{1,0:T(8,128)(2,1)S(1)}, u32[]{:S(2)}, u32[]{:S(2)}) collective-permute-start(bf16[56,2688]{1,0:T(8,128)(2,1)} %get-tuple-element.48), channel_id=1, source_target_pairs={{0,24},{8,16},{16,8},{24,0},{1,25},{9,17},{17,9},{25,1},{2,26},{10... | collective-permute-start | bytes 903176 | tf_op jit(solution)/shard_map/ppermute | solution.py:433
  393.0 16.0 %collective-permute-start.37 = (bf16[56,2688]{1,0:T(8,128)(2,1)}, bf16[56,2688]{1,0:T(8,128)(2,1)S(1)}, u32[]{:S(2)}, u32[]{:S(2)}) collective-permute-start(bf16[56,2688]{1,0:T(8,128)(2,1)} %get-tuple-element.49), channel_id=1, source_target_pairs={{0,16},{8,24},{16,0},{24,8},{1,17},{9,25},{17,1},{25,9},{2,18},{10... | collective-permute-start | bytes 903176 | tf_op jit(solution)/shard_map/ppermute | solution.py:433
  395.3 18.1 %collective-permute-start.65 = (bf16[128,2688]{1,0:T(8,128)(2,1)}, bf16[128,2688]{1,0:T(8,128)(2,1)}, u32[]{:S(2)}, u32[]{:S(2)}) collective-permute-start(bf16[128,2688]{1,0:T(8,128)(2,1)} %get-tuple-element.37), channel_id=1, source_target_pairs={{0,2},{2,4},{4,6},{6,7},{7,5},{5,3},{3,1},{1,0},{8,10},{10,12},{12... | collective-permute-start | bytes 2064392 | tf_op jit(solution)/shard_map/ppermute | solution.py:53
  396.1 17.3 %collective-permute-start.69 = (bf16[128,2688]{1,0:T(8,128)(2,1)S(1)}, bf16[128,2688]{1,0:T(8,128)(2,1)}, u32[]{:S(2)}, u32[]{:S(2)}) collective-permute-start(bf16[128,2688]{1,0:T(8,128)(2,1)S(1)} %get-tuple-element.38), channel_id=1, source_target_pairs={{2,0},{4,2},{6,4},{7,6},{5,7},{3,5},{1,3},{0,1},{10,8},{12,10},{14... | collective-permute-start | bytes 2064392 | tf_op jit(solution)/shard_map/ppermute | solution.py:53
  416.2 17.3 %collective-permute-start.66 = (bf16[128,2688]{1,0:T(8,128)(2,1)}, bf16[128,2688]{1,0:T(8,128)(2,1)}, u32[]{:S(2)}, u32[]{:S(2)}) collective-permute-start(bf16[128,2688]{1,0:T(8,128)(2,1)} %get-tuple-element.35), channel_id=1, source_target_pairs={{0,2},{2,4},{4,6},{6,7},{7,5},{5,3},{3,1},{1,0},{8,10},{10,12},{12... | collective-permute-start | bytes 2064392 | tf_op jit(solution)/shard_map/ppermute | solution.py:53
  416.8 16.7 %collective-permute-start.70 = (bf16[128,2688]{1,0:T(8,128)(2,1)}, bf16[128,2688]{1,0:T(8,128)(2,1)}, u32[]{:S(2)}, u32[]{:S(2)}) collective-permute-start(bf16[128,2688]{1,0:T(8,128)(2,1)} %get-tuple-element.36), channel_id=1, source_target_pairs={{2,0},{4,2},{6,4},{7,6},{5,7},{3,5},{1,3},{0,1},{10,8},{12,10},{14... | collective-permute-start | bytes 2064392 | tf_op jit(solution)/shard_map/ppermute | solution.py:53
  (162 other events, 1475.3 us)
